TPU v7x, 512 devices: a whole 4x8x8 slice. The times are simulated.
512 devices in a mesh: gx: 16 (over z, core), gy: 8 (over y), gz: 4 (over x).
Axes of the slice: x: 4, y: 8, z: 8, core: 2. Of those that a mesh axis runs over, the one named last changes fastest.
Arguments:
- start: float32 [4, 80, 256, 512], P(None, 'gx', 'gy', 'gz'), may hold values from -6 to 6
- rhs_block: float32 [4, 80, 256, 512], P(None, 'gx', 'gy', 'gz'), may hold values from -6 to 6
- coefficients: float32 [4, 80, 256, 512], P(None, 'gx', 'gy', 'gz'), may hold values from 0.5 to 2
Outputs:
- solution: float32 [4, 80, 256, 512], P(None, 'gx', 'gy', 'gz')
All inputs are finite; a program needn't handle non-finite values.
Results may differ from a plain program's by a relative error of at most 0.0003.
Values sent between devices are 32-bit elements; how exact they have to be, the bound alone decides.
A program may use at most 192 MiB of HBM per device.

v0:
```python
import jax
import jax.numpy as jnp
from jax import lax
from jax.sharding import PartitionSpec as P

S = 4


basis_shift = 8.75
basis_scale = 4.0


def padded(block, sides, width):
    for axis, dim in sides:
        count = lax.axis_size(axis)
        forward = [(i, i + 1) for i in range(count - 1)]
        backward = [(target, source) for source, target in forward]
        low = lax.ppermute(
            lax.slice_in_dim(block, block.shape[dim] - width, None, axis=dim), axis, forward
        )
        high = lax.ppermute(lax.slice_in_dim(block, 0, width, axis=dim), axis, backward)
        block = jnp.concatenate([low, block, high], axis=dim)
    return block


def stencil(field, coefs):
    center = field[:, 1:-1, 1:-1, 1:-1]
    result = coefs[0, 1:-1, 1:-1, 1:-1] * center
    result = result + coefs[1, 1:-1, 1:-1, 1:-1] * (center - field[:, 2:, 1:-1, 1:-1])
    result = result + coefs[1, :-2, 1:-1, 1:-1] * (center - field[:, :-2, 1:-1, 1:-1])
    result = result + coefs[2, 1:-1, 1:-1, 1:-1] * (center - field[:, 1:-1, 2:, 1:-1])
    result = result + coefs[2, 1:-1, :-2, 1:-1] * (center - field[:, 1:-1, :-2, 1:-1])
    result = result + coefs[3, 1:-1, 1:-1, 1:-1] * (center - field[:, 1:-1, 1:-1, 2:])
    result = result + coefs[3, 1:-1, 1:-1, :-2] * (center - field[:, 1:-1, 1:-1, :-2])
    return result


def reflect_rows(tall):
    count = tall.shape[0]
    entries = tall.shape[1]
    position = jnp.arange(entries)
    for j in range(count):
        column = jnp.where(position >= j, tall[j], 0.0)
        length = jnp.sqrt(jnp.sum(column * column))
        leading = tall[j, j]
        mirror = -jnp.where(leading >= 0, 1.0, -1.0) * length
        vector = column - mirror * (position == j).astype(jnp.float32)
        weight = jnp.sum(vector * vector)
        project = jnp.dot(tall, vector, precision=lax.Precision.HIGHEST) / weight
        tall = tall - 2.0 * project[:, None] * vector[None, :]
    factor = tall.T
    flip_sign = jnp.where(jnp.diagonal(factor) >= 0, 1.0, -1.0)
    return jnp.triu(factor * flip_sign[:, None])


def back_solve(triangle, values):
    count = triangle.shape[0]
    answer = [None] * count
    for i in reversed(range(count)):
        partial_sum = values[i]
        for j in range(i + 1, count):
            partial_sum = partial_sum - triangle[i, j] * answer[j]
        answer[i] = partial_sum / triangle[i, i]
    return jnp.stack(answer)


def least_squares(upper, nrhs):
    total = upper.shape[0]
    kept = total - nrhs
    rows = jnp.arange(total)[:, None]
    cols = jnp.arange(kept)[None, :]
    shifts = basis_shift * (rows == cols).astype(jnp.float32) + basis_scale * (
        rows == cols + nrhs
    ).astype(jnp.float32)
    mixed = jnp.dot(upper, shifts, precision=lax.Precision.HIGHEST)
    joined = jnp.concatenate([mixed, upper[:, :nrhs]], axis=1)
    reduced = reflect_rows(joined.T)
    return back_solve(reduced[:kept, :kept], reduced[:kept, kept:])


def local(start, rhs_block, coefficients):
    nrhs = start.shape[0]
    guess_ext, coef_ext = (
        padded(start, (("gx", 1), ("gy", 2), ("gz", 3)), 1),
        padded(coefficients, (("gx", 1), ("gy", 2), ("gz", 3)), 1),
    )
    blocks = [rhs_block - stencil(guess_ext, coef_ext)]
    for step in range(S):
        before = blocks[-1]
        widened = padded(before, (("gx", 1), ("gy", 2), ("gz", 3)), 1)
        blocks.append((stencil(widened, coef_ext) - basis_shift * before) / basis_scale)
    tall = jnp.stack(blocks).reshape(len(blocks) * nrhs, -1)
    local_gram = jnp.dot(tall, tall.T, precision=lax.Precision.HIGHEST)
    gram = lax.psum(local_gram, ("gx", "gy", "gz"))
    upper = jnp.linalg.cholesky(gram).T
    weights = least_squares(upper, nrhs)
    kept = tall.shape[0] - nrhs
    update = jnp.dot(weights.T, tall[:kept], precision=lax.Precision.HIGHEST)
    return start + update.reshape(start.shape)


def solution(mesh):
    placed = (P(None, "gx", "gy", "gz"), P(None, "gx", "gy", "gz"), P(None, "gx", "gy", "gz"))
    return jax.shard_map(
        local, mesh=mesh, in_specs=placed, out_specs=P(None, "gx", "gy", "gz"), check_vma=False
    )
```

profile of v0, /device:TPU:1, one launch (start us, length us, event | category | flops | bytes accessed | tf_op | source)
XLA Modules:
  0.0 541.6 jit_solution(3785583033890651326)
XLA Ops:
  0.9 5.5 %collective-permute-start.1 = (f32[4,1,32,128]{3,2,1,0:T(8,128)S(1)}, f32[4,1,32,128]{3,2,1,0:T(8,128)S(1)}, u32[]{:S(2)}, u32[]{:S(2)}) collective-permute-start(f32[4,1,32,128]{3,2,1,0:T(8,128)S(1)} %get-tuple-element.80), channel_id=1, source_target_pairs={{0,32},{32,64},{64,96},{96,128},{128,160},{160,192},{192,224},{224... | collective-permute-start | bytes 196616 | tf_op jit(solution)/shard_map/ppermute | solution.py:18
  6.5 4.7 collective-permute-start.4
  14.0 2.4 collective-permute-start
  24.1 5.2 collective-permute-start.6
  36.0 3.1 collective-permute-start.9
  45.9 4.0 collective-permute-start.10
  50.8 2.4 fusion.42
  60.8 5.3 collective-permute-start.12
  68.8 4.0 collective-permute-start.14
  78.9 4.0 collective-permute-start.16
  90.7 6.2 %collective-permute-start.18 = (f32[4,1,32,128]{3,2,1,0:T(8,128)S(1)}, f32[4,1,32,128]{3,2,1,0:T(8,128)S(1)}, u32[]{:S(2)}, u32[]{:S(2)}) collective-permute-start(f32[4,1,32,128]{3,2,1,0:T(8,128)S(1)} %get-tuple-element.70), channel_id=1, source_target_pairs={{0,32},{32,64},{64,96},{96,128},{128,160},{160,192},{192,224},{224... | collective-permute-start | bytes 196616 | tf_op jit(solution)/shard_map/ppermute | solution.py:18
  99.6 4.5 collective-permute-start.20
  107.2 4.5 collective-permute-start.22
  117.3 5.6 %collective-permute-start.24 = (f32[4,1,32,128]{3,2,1,0:T(8,128)S(1)}, f32[4,1,32,128]{3,2,1,0:T(8,128)S(1)}, u32[]{:S(2)}, u32[]{:S(2)}) collective-permute-start(f32[4,1,32,128]{3,2,1,0:T(8,128)S(1)} %get-tuple-element.68), channel_id=1, source_target_pairs={{0,32},{32,64},{64,96},{96,128},{128,160},{160,192},{192,224},{224... | collective-permute-start | bytes 196616 | tf_op jit(solution)/shard_map/ppermute | solution.py:18
  125.5 4.5 collective-permute-start.26
  133.1 4.5 collective-permute-start.28
  141.2 6.0 %collective-permute-start.30 = (f32[4,1,32,128]{3,2,1,0:T(8,128)S(1)}, f32[4,1,32,128]{3,2,1,0:T(8,128)S(1)}, u32[]{:S(2)}, u32[]{:S(2)}) collective-permute-start(f32[4,1,32,128]{3,2,1,0:T(8,128)S(1)} %get-tuple-element.62), channel_id=1, source_target_pairs={{0,32},{32,64},{64,96},{96,128},{128,160},{160,192},{192,224},{224... | collective-permute-start | bytes 196616 | tf_op jit(solution)/shard_map/ppermute | solution.py:18
  149.9 5.5 %collective-permute-start.32 = (f32[4,7,1,128]{3,0,2,1:T(4,128)S(1)}, f32[4,7,1,128]{3,0,2,1:T(4,128)S(1)}, u32[]{:S(2)}, u32[]{:S(2)}) collective-permute-start(f32[4,7,1,128]{3,0,2,1:T(4,128)S(1)} %copy.517), channel_id=1, source_target_pairs={{0,4},{4,8},{8,12},{12,16},{16,20},{20,24},{24,28},{1,5},{5,9},{9,... | collective-permute-start | bytes 43016 | tf_op jit(solution)/shard_map/ppermute | solution.py:18
  159.0 5.1 collective-permute-start.34
  171.2 2.2 fusion.49
  177.3 116.5 %psum.7 = f32[20,20]{0,1:T(8,128)S(1)} all-reduce(f32[20,20]{0,1:T(8,128)S(1)} %fusion.311), channel_id=1, replica_groups=mesh['gx'=16,'gy'=8,'gz'=4] {'gx','gy','gz'}, use_global_device_ids=true, to_apply=%region_0.0 | all-reduce | flops 400 | bytes 3200 | tf_op jit(solution)/shard_map/psum | solution.py:94
  395.1 65.5 %subtract_divide_fusion = (f32[1,4]{1,0:T(1,128)S(1)}, f32[1,4]{1,0:T(1,128)S(1)}, f32[1,4]{1,0:T(1,128)S(1)}, f32[1,4]{1,0:T(1,128)S(1)}, f32[1,4]{1,0:T(1,128)...) fusion(f32[20,20]{1,0:T(8,128)S(1)} %multiply_select_fusion, ...), kind=kLoop, calls=%fused_computation.602 | loop fusion | flops 784 | bytes 884 | tf_op jit(solution)/shard_map/div | solution.py:63
  461.0 57.8 %fusion.191 = (f32[4]{0:T(128)S(1)}, f32[4]{0:T(128)S(1)}, f32[4]{0:T(128)S(1)}, f32[4]{0:T(128)S(1)}, f32[4]{0:T(128)S(1)}, /*index=5*/f32[4]{0:T(128)S(1)}, f3...) fusion(f32[20,20]{1,0:T(8,128)S(1)} %multiply_select_fusion, f32[1,4]{1,0:T(1,128)S(1)} %get-tuple-element.16, ...), kind=kLoop, calls=%fused_computation.504 | loop fusion | flops 704 | bytes 756 | tf_op jit(solution)/shard_map/div | solution.py:63
  518.8 19.3 %fusion.244 = (f32[1,4]{1,0:T(1,128)S(1)}, f32[4]{0:T(128)S(1)}) fusion(f32[1,4]{1,0:T(1,128)S(1)} %get-tuple-element.19, f32[1,4]{1,0:T(1,128)S(1)} %get-tuple-element.18, f32[1,4]{1,0:T(1,128)S(1)} %get-tuple-element.17, f32[1,4]{1,0:T(1,128)S(1)} %get-tuple-element.16, f32[4]{0:T(128)S(1)} %get-tuple-element.31, f32[4]{0:T(128)S(1)} %get-tuple-element.30, ...), kind=kLoop, calls=%fused_computation.656 | loop fusion | flops 240 | bytes 412 | tf_op jit(solution)/shard_map/stack | solution.py:64
  (378 shorter events, 163.8 us)
Async XLA Ops:
  0.9 15.5 %collective-permute-start.1 = (f32[4,1,32,128]{3,2,1,0:T(8,128)S(1)}, f32[4,1,32,128]{3,2,1,0:T(8,128)S(1)}, u32[]{:S(2)}, u32[]{:S(2)}) collective-permute-start(f32[4,1,32,128]{3,2,1,0:T(8,128)S(1)} %get-tuple-element.80), channel_id=1, source_target_pairs={{0,32},{32,64},{64,96},{96,128},{128,160},{160,192},{192,224},{224... | collective-permute-start | bytes 196616 | tf_op jit(solution)/shard_map/ppermute | solution.py:18
  6.5 11.0 %collective-permute-start.4 = (f32[4,1,32,128]{3,2,1,0:T(8,128)S(1)}, f32[4,1,32,128]{3,2,1,0:T(8,128)S(1)}, u32[]{:S(2)}, u32[]{:S(2)}) collective-permute-start(f32[4,1,32,128]{3,2,1,0:T(8,128)S(1)} %get-tuple-element.79), channel_id=1, source_target_pairs={{32,0},{64,32},{96,64},{128,96},{160,128},{192,160},{224,192},{256... | collective-permute-start | bytes 196616 | tf_op jit(solution)/shard_map/ppermute | solution.py:21
  12.1 9.3 %collective-permute-start.2 = (f32[4,1,32,128]{3,2,1,0:T(8,128)S(1)}, f32[4,1,32,128]{3,2,1,0:T(8,128)S(1)}, u32[]{:S(2)}, u32[]{:S(2)}) collective-permute-start(f32[4,1,32,128]{3,2,1,0:T(8,128)S(1)} %get-tuple-element.82), channel_id=1, source_target_pairs={{0,32},{32,64},{64,96},{96,128},{128,160},{160,192},{192,224},{224... | collective-permute-start | bytes 196616 | tf_op jit(solution)/shard_map/ppermute | solution.py:18
  14.0 7.5 %collective-permute-start = (f32[4,1,32,128]{3,2,1,0:T(8,128)S(1)}, f32[4,1,32,128]{3,2,1,0:T(8,128)S(1)}, u32[]{:S(2)}, u32[]{:S(2)}) collective-permute-start(f32[4,1,32,128]{3,2,1,0:T(8,128)S(1)} %get-tuple-element.81), channel_id=1, source_target_pairs={{32,0},{64,32},{96,64},{128,96},{160,128},{192,160},{224,192},{256... | collective-permute-start | bytes 196616 | tf_op jit(solution)/shard_map/ppermute | solution.py:21
  18.4 12.8 %collective-permute-start.5 = (f32[4,7,1,128]{3,1,2,0:T(8,128)}, f32[4,7,1,128]{3,1,2,0:T(8,128)S(1)}, u32[]{:S(2)}, u32[]{:S(2)}) collective-permute-start(f32[4,7,1,128]{3,1,2,0:T(8,128)} %get-tuple-element.50), channel_id=1, source_target_pairs={{0,4},{4,8},{8,12},{12,16},{16,20},{20,24},{24,28},{1,5},{5,9},{9,... | collective-permute-start | bytes 43016 | tf_op jit(solution)/shard_map/ppermute | solution.py:18
  20.1 13.1 %collective-permute-start.8 = (f32[4,7,1,128]{3,1,2,0:T(8,128)}, f32[4,7,1,128]{3,1,2,0:T(8,128)S(1)}, u32[]{:S(2)}, u32[]{:S(2)}) collective-permute-start(f32[4,7,1,128]{3,1,2,0:T(8,128)} %get-tuple-element.51), channel_id=1, source_target_pairs={{4,0},{8,4},{12,8},{16,12},{20,16},{24,20},{28,24},{5,1},{9,5},{13... | collective-permute-start | bytes 43016 | tf_op jit(solution)/shard_map/ppermute | solution.py:21
  22.2 16.9 %collective-permute-start.3 = (f32[4,7,1,128]{3,0,2,1:T(4,128)}, f32[4,7,1,128]{3,0,2,1:T(4,128)}, u32[]{:S(2)}, u32[]{:S(2)}) collective-permute-start(f32[4,7,1,128]{3,0,2,1:T(4,128)} %copy.550), channel_id=1, source_target_pairs={{4,0},{8,4},{12,8},{16,12},{20,16},{24,20},{28,24},{5,1},{9,5},{13... | collective-permute-start | bytes 43016 | tf_op jit(solution)/shard_map/ppermute | solution.py:21
  24.1 15.8 %collective-permute-start.6 = (f32[4,7,1,128]{3,0,2,1:T(4,128)}, f32[4,7,1,128]{3,0,2,1:T(4,128)}, u32[]{:S(2)}, u32[]{:S(2)}) collective-permute-start(f32[4,7,1,128]{3,0,2,1:T(4,128)} %copy.551), channel_id=1, source_target_pairs={{0,4},{4,8},{8,12},{12,16},{16,20},{20,24},{24,28},{1,5},{5,9},{9,... | collective-permute-start | bytes 43016 | tf_op jit(solution)/shard_map/ppermute | solution.py:18
  36.0 14.8 %collective-permute-start.9 = (f32[4,7,34,1]{2,1,3,0:T(8,128)S(1)}, f32[4,7,34,1]{2,1,3,0:T(8,128)S(1)}, u32[]{:S(2)}, u32[]{:S(2)}) collective-permute-start(f32[4,7,34,1]{2,1,3,0:T(8,128)S(1)} %pad_maximum_fusion.93), channel_id=1, source_target_pairs={{0,1},{1,2},{2,3},{4,5},{5,6},{6,7},{8,9},{9,10},{10,11},{12,13},{... | collective-permute-start | bytes 11432 | tf_op jit(solution)/shard_map/ppermute | solution.py:18
  43.2 11.2 %collective-permute-start.7 = (f32[4,7,34,1]{2,0,3,1:T(4,128)S(1)}, f32[4,7,34,1]{2,0,3,1:T(4,128)S(1)}, u32[]{:S(2)}, u32[]{:S(2)}) collective-permute-start(f32[4,7,34,1]{2,0,3,1:T(4,128)S(1)} %copy.476), channel_id=1, source_target_pairs={{1,0},{2,1},{3,2},{5,4},{6,5},{7,6},{9,8},{10,9},{11,10},{13,12},{... | collective-permute-start | bytes 11432 | tf_op jit(solution)/shard_map/ppermute | solution.py:21
  45.9 9.7 %collective-permute-start.10 = (f32[4,7,34,1]{2,0,3,1:T(4,128)S(1)}, f32[4,7,34,1]{2,0,3,1:T(4,128)S(1)}, u32[]{:S(2)}, u32[]{:S(2)}) collective-permute-start(f32[4,7,34,1]{2,0,3,1:T(4,128)S(1)} %copy.483), channel_id=1, source_target_pairs={{0,1},{1,2},{2,3},{4,5},{5,6},{6,7},{8,9},{9,10},{10,11},{12,13},{... | collective-permute-start | bytes 11432 | tf_op jit(solution)/shard_map/ppermute | solution.py:18
  58.9 7.3 %collective-permute-start.11 = (f32[4,1,32,128]{3,2,1,0:T(8,128)S(1)}, f32[4,1,32,128]{3,2,1,0:T(8,128)S(1)}, u32[]{:S(2)}, u32[]{:S(2)}) collective-permute-start(f32[4,1,32,128]{3,2,1,0:T(8,128)S(1)} %get-tuple-element.73), channel_id=1, source_target_pairs={{32,0},{64,32},{96,64},{128,96},{160,128},{192,160},{224,192},{256... | collective-permute-start | bytes 196616 | tf_op jit(solution)/shard_map/ppermute | solution.py:21
  60.8 6.6 %collective-permute-start.12 = (f32[4,1,32,128]{3,2,1,0:T(8,128)S(1)}, f32[4,1,32,128]{3,2,1,0:T(8,128)S(1)}, u32[]{:S(2)}, u32[]{:S(2)}) collective-permute-start(f32[4,1,32,128]{3,2,1,0:T(8,128)S(1)} %get-tuple-element.72), channel_id=1, source_target_pairs={{0,32},{32,64},{64,96},{96,128},{128,160},{160,192},{192,224},{224... | collective-permute-start | bytes 196616 | tf_op jit(solution)/shard_map/ppermute | solution.py:18
  76.2 6.6 %collective-permute-start.15 = (f32[4,7,34,1]{2,0,3,1:T(4,128)S(1)}, f32[4,7,34,1]{2,0,3,1:T(4,128)S(1)}, u32[]{:S(2)}, u32[]{:S(2)}) collective-permute-start(f32[4,7,34,1]{2,0,3,1:T(4,128)S(1)} %copy.491), channel_id=1, source_target_pairs={{1,0},{2,1},{3,2},{5,4},{6,5},{7,6},{9,8},{10,9},{11,10},{13,12},{... | collective-permute-start | bytes 11432 | tf_op jit(solution)/shard_map/ppermute | solution.py:21
  88.8 8.2 %collective-permute-start.17 = (f32[4,1,32,128]{3,2,1,0:T(8,128)S(1)}, f32[4,1,32,128]{3,2,1,0:T(8,128)S(1)}, u32[]{:S(2)}, u32[]{:S(2)}) collective-permute-start(f32[4,1,32,128]{3,2,1,0:T(8,128)S(1)} %get-tuple-element.71), channel_id=1, source_target_pairs={{32,0},{64,32},{96,64},{128,96},{160,128},{192,160},{224,192},{256... | collective-permute-start | bytes 196616 | tf_op jit(solution)/shard_map/ppermute | solution.py:21
  90.7 7.5 %collective-permute-start.18 = (f32[4,1,32,128]{3,2,1,0:T(8,128)S(1)}, f32[4,1,32,128]{3,2,1,0:T(8,128)S(1)}, u32[]{:S(2)}, u32[]{:S(2)}) collective-permute-start(f32[4,1,32,128]{3,2,1,0:T(8,128)S(1)} %get-tuple-element.70), channel_id=1, source_target_pairs={{0,32},{32,64},{64,96},{96,128},{128,160},{160,192},{192,224},{224... | collective-permute-start | bytes 196616 | tf_op jit(solution)/shard_map/ppermute | solution.py:18
  105.6 7.0 %collective-permute-start.21 = (f32[4,7,34,1]{2,0,3,1:T(4,128)S(1)}, f32[4,7,34,1]{2,0,3,1:T(4,128)S(1)}, u32[]{:S(2)}, u32[]{:S(2)}) collective-permute-start(f32[4,7,34,1]{2,0,3,1:T(4,128)S(1)} %copy.501), channel_id=1, source_target_pairs={{1,0},{2,1},{3,2},{5,4},{6,5},{7,6},{9,8},{10,9},{11,10},{13,12},{... | collective-permute-start | bytes 11432 | tf_op jit(solution)/shard_map/ppermute | solution.py:21
  115.3 7.5 %collective-permute-start.23 = (f32[4,1,32,128]{3,2,1,0:T(8,128)S(1)}, f32[4,1,32,128]{3,2,1,0:T(8,128)S(1)}, u32[]{:S(2)}, u32[]{:S(2)}) collective-permute-start(f32[4,1,32,128]{3,2,1,0:T(8,128)S(1)} %get-tuple-element.69), channel_id=1, source_target_pairs={{32,0},{64,32},{96,64},{128,96},{160,128},{192,160},{224,192},{256... | collective-permute-start | bytes 196616 | tf_op jit(solution)/shard_map/ppermute | solution.py:21
  117.3 6.9 %collective-permute-start.24 = (f32[4,1,32,128]{3,2,1,0:T(8,128)S(1)}, f32[4,1,32,128]{3,2,1,0:T(8,128)S(1)}, u32[]{:S(2)}, u32[]{:S(2)}) collective-permute-start(f32[4,1,32,128]{3,2,1,0:T(8,128)S(1)} %get-tuple-element.68), channel_id=1, source_target_pairs={{0,32},{32,64},{64,96},{96,128},{128,160},{160,192},{192,224},{224... | collective-permute-start | bytes 196616 | tf_op jit(solution)/shard_map/ppermute | solution.py:18
  139.3 7.9 %collective-permute-start.29 = (f32[4,1,32,128]{3,2,1,0:T(8,128)S(1)}, f32[4,1,32,128]{3,2,1,0:T(8,128)S(1)}, u32[]{:S(2)}, u32[]{:S(2)}) collective-permute-start(f32[4,1,32,128]{3,2,1,0:T(8,128)S(1)} %get-tuple-element.63), channel_id=1, source_target_pairs={{32,0},{64,32},{96,64},{128,96},{160,128},{192,160},{224,192},{256... | collective-permute-start | bytes 196616 | tf_op jit(solution)/shard_map/ppermute | solution.py:21
  141.2 7.3 %collective-permute-start.30 = (f32[4,1,32,128]{3,2,1,0:T(8,128)S(1)}, f32[4,1,32,128]{3,2,1,0:T(8,128)S(1)}, u32[]{:S(2)}, u32[]{:S(2)}) collective-permute-start(f32[4,1,32,128]{3,2,1,0:T(8,128)S(1)} %get-tuple-element.62), channel_id=1, source_target_pairs={{0,32},{32,64},{64,96},{96,128},{128,160},{160,192},{192,224},{224... | collective-permute-start | bytes 196616 | tf_op jit(solution)/shard_map/ppermute | solution.py:18
  148.6 7.5 %collective-permute-start.31 = (f32[4,7,1,128]{3,0,2,1:T(4,128)S(1)}, f32[4,7,1,128]{3,0,2,1:T(4,128)S(1)}, u32[]{:S(2)}, u32[]{:S(2)}) collective-permute-start(f32[4,7,1,128]{3,0,2,1:T(4,128)S(1)} %copy.515), channel_id=1, source_target_pairs={{4,0},{8,4},{12,8},{16,12},{20,16},{24,20},{28,24},{5,1},{9,5},{13... | collective-permute-start | bytes 43016 | tf_op jit(solution)/shard_map/ppermute | solution.py:21
  156.8 11.5 %collective-permute-start.33 = (f32[4,7,34,1]{2,0,3,1:T(4,128)S(1)}, f32[4,7,34,1]{2,0,3,1:T(4,128)}, u32[]{:S(2)}, u32[]{:S(2)}) collective-permute-start(f32[4,7,34,1]{2,0,3,1:T(4,128)S(1)} %copy.521), channel_id=1, source_target_pairs={{1,0},{2,1},{3,2},{5,4},{6,5},{7,6},{9,8},{10,9},{11,10},{13,12},{... | collective-permute-start | bytes 11432 | tf_op jit(solution)/shard_map/ppermute | solution.py:21
  159.0 10.4 %collective-permute-start.34 = (f32[4,7,34,1]{2,0,3,1:T(4,128)}, f32[4,7,34,1]{2,0,3,1:T(4,128)}, u32[]{:S(2)}, u32[]{:S(2)}) collective-permute-start(f32[4,7,34,1]{2,0,3,1:T(4,128)} %copy.523), channel_id=1, source_target_pairs={{0,1},{1,2},{2,3},{4,5},{5,6},{6,7},{8,9},{9,10},{10,11},{12,13},{... | collective-permute-start | bytes 11432 | tf_op jit(solution)/shard_map/ppermute | solution.py:18
  (37 other events, 719.0 us)
where the time goes:
time: 546 us; the launch traced here: 542 us
  other arithmetic  195 us (36%)
  blocking collectives  116 us (21%)
  starting transfers between devices  110 us (20%)
  local copies, waits for them, and re-layouts  62.4 us (11%)
  between operations  29.3 us (5%)
  matrix products  20.1 us (4%)
  waiting for transfers between devices  8.15 us (1%)
    div x2, other arithmetic, back_solve(): answer[i] = partial_sum / triangle[i, i]  123 us
    psum x1, blocking collectives, local(): gram = lax.psum(local_gram, ('gx', 'gy', 'gz'))  116 us
    ppermute x18, starting transfers between devices, padded(): lax.ppermute(lax.slice_in_dim(block, block.shape[dim] - width, None, axis...  81.2 us
    ppermute x17, starting transfers between devices, padded(): lax.ppermute(lax.slice_in_dim(block, 0, width, axis=dim), axis, backward)  28.9 us
    another operation x1, other arithmetic, back_solve(): return jnp.stack(answer)  19.3 us
    dot_general x20, matrix products, reflect_rows(): project = jnp.dot(tall, vector, precision=lax.Precision.HIGHEST) / weight  15.7 us
    reduce_sum x20, other arithmetic, reflect_rows(): length = jnp.sqrt(jnp.sum(column * column))  13.6 us
    reduce_sum x20, other arithmetic, reflect_rows(): weight = jnp.sum(vector * vector)  12 us
  transfers between devices with their start and end apart: 35, of which 8 were waited for; matrix products, arithmetic and copies ran while one was open for 6% of the time, Pallas kernels for 0%

commit v1 on v0

v1 whole, which is shorter than its diff:
```python
import itertools

import jax
import jax.numpy as jnp
from jax import lax
from jax.experimental import pallas as pl
from jax.experimental.pallas import tpu as pltpu
from jax.sharding import PartitionSpec as P

MESH = pl.DeviceIdType.MESH
F32 = jnp.float32
HIGH = lax.Precision.HIGHEST
AXES = ("gx", "gy", "gz")
SHIFT, SCALE = 8.75, 4.0
PAIRS = [(i, j) for i in range(4) for j in range(i, 4)]
PLACE = {(i, j): PAIRS.index((min(i, j), max(i, j))) for i in range(4) for j in range(4)}
TOP = 8
XLO, XHI, YLO, YHI, ZLO, ZHI, CX = range(7)


def rolled(tile, shift):
    return pltpu.roll(tile, shift % 128, 1)


def kernel(
    sizes, start, rhs, coef, out,
    V, rhs_v, coef_v, bd, bc1, bc2, bc3p, bc3m, e3, e1, e2,
    xh, c1h, ys, yr, zs, zr, G, row_a, row_b, msg, rep, W,
    lsem, ssem, rsem, asem,
):
    nx, ny, nz = sizes
    me = [lax.axis_index(axis) for axis in AXES]

    def shifted(offset):
        return tuple(lax.rem(m + (d + s), s) for m, d, s in zip(me, offset, sizes))

    neighbours = [shifted(o) for o in ((1, 0, 0), (-1, 0, 0), (0, 1, 0), (0, -1, 0), (0, 0, 1), (0, 0, -1))]

    def far(o):
        return -sum(min(d, s - d) for d, s in zip(o, sizes))

    plane = sorted([(0, b, c) for b, c in itertools.product(range(ny), range(nz)) if b or c], key=far)
    line = sorted([(a, 0, 0) for a in range(1, nx)], key=far)

    loads = [
        pltpu.make_async_copy(start.at[f], V.at[0, :, f, pl.ds(TOP, 32), :], lsem.at[f]) for f in range(4)
    ] + [pltpu.make_async_copy(coef, coef_v, lsem.at[4]), pltpu.make_async_copy(rhs, rhs_v, lsem.at[5])]
    for copy in loads:
        copy.start()

    barrier = pltpu.get_barrier_semaphore()
    partners = [shifted(o) for o in plane + line]
    for partner in partners:
        pl.semaphore_signal(barrier, inc=1, device_id=partner, device_id_type=MESH)

    lane = lax.broadcasted_iota(jnp.int32, (8, 128), 1)
    sub = lax.broadcasted_iota(jnp.int32, (8, 128), 0)
    pair_lane = lax.shift_right_logical(lane, 1)
    even_lane = lax.rem(lane, 2) == 0
    zero = jnp.zeros((8, 128), F32)

    def inside(axis, edge):
        return jnp.where(me[axis] == edge, 0.0, 1.0).astype(F32)

    low = [inside(0, 0), inside(1, 0), inside(2, 0)]
    high = [inside(0, nx - 1), inside(1, ny - 1), inside(2, nz - 1)]

    def clear(i, carry):
        for f in range(4):
            for x in range(5):
                V[i, x, f, pl.ds(0, 8), :] = zero
                V[i, x, f, pl.ds(TOP + 32, 8), :] = zero
        return carry

    lax.fori_loop(0, 5, clear, 0)
    for x in range(5):
        bc2[x, pl.ds(0, 8), :] = zero
    G[pl.ds(96, 32), :] = jnp.zeros((32, 128), F32)

    loads[4].wait()

    for x in range(5):
        for t in range(4):
            rows = pl.ds(8 * t, 8)
            bc2[x, pl.ds(TOP + 8 * t, 8), :] = -0.25 * coef_v[2, x, rows, :]
        for t in range(4):
            rows = pl.ds(8 * t, 8)
            n1 = -0.25 * coef_v[1, x, rows, :]
            n3 = -0.25 * coef_v[3, x, rows, :]
            bc1[x, rows, :] = n1
            bc3p[x, rows, :] = jnp.where(lane == 127, 0.0, n3)
            back = jnp.where(lane == 0, 0.0, rolled(n3, 1))
            bc3m[x, rows, :] = back
            e3[x, rows, :] = jnp.where(lane == 127, n3 * high[2], 0.0)
            total = n1 + n3 + back + bc2[x, pl.ds(TOP + 8 * t, 8), :] + bc2[x, pl.ds(TOP - 1 + 8 * t, 8), :]
            if x > 0:
                total = total + bc1[x - 1, rows, :]
            bd[x, rows, :] = 0.25 * (coef_v[0, x, rows, :] - SHIFT) - total
            if x == 4:
                e1[1, rows, :] = n1 * high[0]
        e2[1, x, :, :] = jnp.where(sub == 7, bc2[x, pl.ds(TOP + 24, 8), :] * high[1], 0.0)

    def x_copies(p):
        return [
            pltpu.make_async_remote_copy(
                V.at[p, 4, :, pl.ds(TOP, 32), :], xh.at[p, 0], ssem.at[p, XLO], rsem.at[p, XLO],
                device_id=neighbours[0], device_id_type=MESH),
            pltpu.make_async_remote_copy(
                V.at[p, 0, :, pl.ds(TOP, 32), :], xh.at[p, 1], ssem.at[p, XHI], rsem.at[p, XHI],
                device_id=neighbours[1], device_id_type=MESH),
        ]

    def yz_copies(p):
        return [
            pltpu.make_async_remote_copy(
                ys.at[p, d], yr.at[p, d], ssem.at[p, YLO + d], rsem.at[p, YLO + d],
                device_id=neighbours[2 + d], device_id_type=MESH) for d in range(2)
        ] + [
            pltpu.make_async_remote_copy(
                zs.at[p], zr.at[p, d], ssem.at[p, ZLO + d], rsem.at[p, ZLO + d],
                device_id=neighbours[4 + d], device_id_type=MESH) for d in range(2)
        ]

    c_copy = pltpu.make_async_remote_copy(
        coef_v.at[1, 4], c1h, ssem.at[0, CX], rsem.at[0, CX], device_id=neighbours[0], device_id_type=MESH
    )

    def begin(copies):
        for copy in copies:
            copy.start()

    def pack(tile, spot, t, held):
        k = 2 * spot + t % 2
        held[t // 2] = jnp.where(pair_lane == k, rolled(tile, 2 * k + 1), held[t // 2])

    for copy in loads[:4]:
        copy.wait()
    held = [zero, zero]
    for x in range(5):
        for f in range(4):
            j = 4 * x + f
            ys[0, 0, pl.ds(j, 1), :] = V[0, x, f, pl.ds(TOP + 31, 1), :]
            ys[0, 1, pl.ds(j, 1), :] = V[0, x, f, pl.ds(TOP, 1), :]
            for t in range(4):
                pack(V[0, x, f, pl.ds(TOP + 8 * t, 8), :], j, t, held)
        ys[0, 0, pl.ds(20 + x, 1), :] = coef_v[2, x, pl.ds(31, 1), :]
        ys[0, 1, pl.ds(20 + x, 1), :] = coef_v[2, x, pl.ds(31, 1), :]
        for t in range(4):
            pack(coef_v[3, x, pl.ds(8 * t, 8), :], 20 + x, t, held)
    for h in range(2):
        zs[0, pl.ds(8 * h, 8), :] = held[h]

    pl.semaphore_wait(barrier, len(partners))
    begin(x_copies(0) + [c_copy] + yz_copies(0))

    def interior(p):
        def layer(x, below, above):
            for t in range(4):
                rows = pl.ds(8 * t, 8)
                c_d, c_xp = bd[x, rows, :], bc1[x, rows, :]
                c_yp, c_ym = bc2[x, pl.ds(TOP + 8 * t, 8), :], bc2[x, pl.ds(TOP - 1 + 8 * t, 8), :]
                c_zp, c_zm = bc3p[x, rows, :], bc3m[x, rows, :]
                for f in range(4):
                    v = V[p, x, f, pl.ds(TOP + 8 * t, 8), :]
                    total = c_d * v
                    total = total + c_yp * V[p, x, f, pl.ds(TOP + 1 + 8 * t, 8), :]
                    total = total + c_ym * V[p, x, f, pl.ds(TOP - 1 + 8 * t, 8), :]
                    if above:
                        total = total + c_xp * V[p, x + 1, f, pl.ds(TOP + 8 * t, 8), :]
                    if below:
                        total = total + bc1[x - 1, rows, :] * V[p, x - 1, f, pl.ds(TOP + 8 * t, 8), :]
                    total = total + c_zp * rolled(v, -1)
                    total = total + c_zm * rolled(v, 1)
                    V[p + 1, x, f, pl.ds(TOP + 8 * t, 8), :] = total

        layer(0, False, True)

        def middle(x, carry):
            layer(x, True, True)
            return carry

        lax.fori_loop(1, 4, middle, 0)
        layer(4, True, False)

    def products(p):
        def layer(x, sums):
            sums = list(sums)
            for t in range(4):
                new = [V[p, x, f, pl.ds(TOP + 8 * t, 8), :] for f in range(4)]
                old = [V[p - 1, x, f, pl.ds(TOP + 8 * t, 8), :] for f in range(4)]
                for q, (i, j) in enumerate(PAIRS):
                    sums[q] = sums[q] + old[i] * new[j]
                    sums[10 + q] = sums[10 + q] + new[i] * new[j]
            return tuple(sums)

        sums = lax.fori_loop(0, 5, layer, (zero,) * 20)
        for q in range(20):
            G[pl.ds(20 * p - 20 + q, 1), :] = jnp.sum(sums[q], axis=0, keepdims=True)

    def finish(p, first=False, last=False):
        for copy in x_copies(p) + yz_copies(p) + ([c_copy] if first else []):
            copy.wait_recv()
        both = [
            jnp.where(even_lane, zr[p, 0, pl.ds(8 * h, 8), :], rolled(zr[p, 1, pl.ds(8 * h, 8), :], -2))
            for h in range(2)
        ]
        held = [zero, zero]
        for x in (0, 4, 1, 2, 3):
            for t in range(4):
                rows = pl.ds(8 * t, 8)
                edge = e3[x, rows, :]
                if first:
                    k = 2 * (20 + x) + t % 2
                    more = jnp.where(lane == 0, (-0.25 * low[2]) * rolled(both[t // 2], -2 * k), 0.0)
                    edge = edge + more
                    e3[x, rows, :] = edge
                    if x == 0:
                        face = (-0.25 * low[0]) * c1h[rows, :]
                        e1[0, rows, :] = face
                        more = more + face
                    if t == 0:
                        row = jnp.broadcast_to(yr[p, 0, pl.ds(20 + x, 1), :], (8, 128))
                        face = jnp.where(sub == 0, (-0.25 * low[1]) * row, 0.0)
                        e2[0, x, :, :] = face
                        more = more + face
                    bd[x, rows, :] = bd[x, rows, :] - more
                for f in range(4):
                    j = 4 * x + f
                    k = 2 * j + t % 2
                    cells = pl.ds(TOP + 8 * t, 8)
                    total = V[p + 1, x, f, cells, :]
                    if x == 0:
                        total = total + e1[0, rows, :] * xh[p, 0, f, rows, :]
                    if x == 4:
                        total = total + e1[1, rows, :] * xh[p, 1, f, rows, :]
                    if t == 0:
                        total = total + e2[0, x, :, :] * jnp.broadcast_to(yr[p, 0, pl.ds(j, 1), :], (8, 128))
                    if t == 3:
                        total = total + e2[1, x, :, :] * jnp.broadcast_to(yr[p, 1, pl.ds(j, 1), :], (8, 128))
                    total = total + edge * rolled(both[t // 2], -2 * k)
                    if first:
                        v = V[p, x, f, cells, :]
                        total = total - more * v
                        total = rhs_v[f, x, rows, :] - SHIFT * v - SCALE * total
                    V[p + 1, x, f, cells, :] = total
                    if not last:
                        if t == 3:
                            ys[p + 1, 0, pl.ds(j, 1), :] = total[7:8, :]
                        if t == 0:
                            ys[p + 1, 1, pl.ds(j, 1), :] = total[0:1, :]
                        pack(total, j, t, held)
            if x == 4 and not last:
                begin(x_copies(p + 1))
        if not last:
            for h in range(2):
                zs[p + 1, pl.ds(8 * h, 8), :] = held[h]
            begin(yz_copies(p + 1))

    interior(0)
    loads[5].wait()
    finish(0, first=True)

    def power(p, carry):
        interior(p)
        products(p)
        finish(p)
        return carry

    lax.fori_loop(1, 4, power, 0)
    interior(4)
    products(4)
    finish(4, last=True)
    products(5)

    ones = jnp.ones((8, 128), F32)

    def everyone(row, offsets, rows_ref, mine, count, slot):
        msg[slot, :, :] = row
        copies = [
            pltpu.make_async_remote_copy(
                msg.at[slot, pl.ds(0, 1), :], rows_ref.at[pl.ds(mine, 1), :], asem.at[slot, 0], asem.at[slot, 1],
                device_id=shifted(o), device_id_type=MESH) for o in offsets
        ]
        begin(copies)
        others = rows_ref.at[pl.ds(0, count - 1), :]
        pltpu.make_async_copy(others, others, asem.at[slot, 1]).wait()
        total = None
        for r in range(count // 8):
            part = jnp.where(sub + 8 * r == mine, row, rows_ref[pl.ds(8 * r, 8), :])
            total = part if total is None else total + part
        return jnp.broadcast_to(jnp.sum(total, axis=0, keepdims=True), (8, 128))

    def sent(rows_ref, count, slot):
        others = rows_ref.at[pl.ds(0, count - 1), :]
        pltpu.make_async_copy(others, others, asem.at[slot, 0]).wait()

    g = lax.dot_general(ones, G[...], (((1,), (1,)), ((), ())), precision=HIGH, preferred_element_type=F32)
    g = everyone(g, plane, row_a, me[1] * nz + me[2], ny * nz, 0)
    g = everyone(g, line, row_b, me[0], nx, 1)

    ahead, after = rolled(g, -10), rolled(g, -20)
    normal = (SHIFT * SHIFT) * g + (2 * SHIFT * SCALE) * ahead + (SCALE * SCALE) * after
    right = SHIFT * g + SCALE * ahead
    entries = jnp.where(lane < 80, normal, rolled(right, 70))
    spread = jnp.concatenate([jnp.where(sub + 8 * r == lane, entries, 0.0) for r in range(16)], axis=0)
    rep[...] = lax.dot_general(
        spread, jnp.ones((128, 128), F32), (((1,), (0,)), ((), ())), precision=HIGH, preferred_element_type=F32
    )

    def entry(r):
        return jnp.broadcast_to(rep[pl.ds(r, 1), :], (8, 128))

    n = 16
    a = {}
    for i in range(n):
        for j in range(i + 1):
            a[i, j] = entry(10 * (i // 4 + j // 4 + 1) + PLACE[i % 4, j % 4])
    b = []
    for i in range(n):
        value = entry(80 + 10 * (i // 4) + PLACE[i % 4, 3])
        for j in range(3):
            value = jnp.where(sub == j, entry(80 + 10 * (i // 4) + PLACE[i % 4, j]), value)
        b.append(value)
    inverse = []
    for k in range(n):
        inverse.append(1.0 / a[k, k])
        for i in range(k + 1, n):
            factor = a[i, k] * inverse[k]
            for j in range(k + 1, i + 1):
                a[i, j] = a[i, j] - factor * a[j, k]
            b[i] = b[i] - factor * b[k]
    for i in reversed(range(n)):
        b[i] = b[i] * inverse[i]
        W[i, :, :] = b[i]
        for j in range(i):
            b[j] = b[j] - a[i, j] * b[i]

    def update(x, carry):
        total = [[V[0, x, f, pl.ds(TOP + 8 * t, 8), :] for t in range(4)] for f in range(4)]
        for c in range(16):
            v = [V[1 + c // 4, x, c % 4, pl.ds(TOP + 8 * t, 8), :] for t in range(4)]
            for f in range(4):
                w = jnp.broadcast_to(W[c, pl.ds(f, 1), :], (8, 128))
                for t in range(4):
                    total[f][t] = total[f][t] + w * v[t]
        for f in range(4):
            for t in range(4):
                out[f, x, pl.ds(8 * t, 8), :] = total[f][t]
        return carry

    lax.fori_loop(0, 5, update, 0)

    for p in range(5):
        for copy in x_copies(p) + yz_copies(p):
            copy.wait_send()
    c_copy.wait_send()
    sent(row_a, ny * nz, 0)
    sent(row_b, nx, 1)


def solution(mesh):
    sizes = tuple(mesh.shape[axis] for axis in AXES)
    spec = P(None, "gx", "gy", "gz")

    def local(start, rhs_block, coefficients):
        vmem = lambda *shape: pltpu.VMEM(shape, F32)
        return pl.pallas_call(
            lambda *refs: kernel(sizes, *refs),
            out_shape=jax.ShapeDtypeStruct(start.shape, F32),
            in_specs=[pl.BlockSpec(memory_space=pl.ANY)] * 3,
            out_specs=pl.BlockSpec(memory_space=pltpu.VMEM),
            scratch_shapes=[
                vmem(6, 5, 4, 48, 128), vmem(4, 5, 32, 128), vmem(4, 5, 32, 128),
                vmem(5, 32, 128), vmem(5, 32, 128), vmem(5, 48, 128),
                vmem(5, 32, 128), vmem(5, 32, 128), vmem(5, 32, 128),
                vmem(2, 32, 128), vmem(2, 5, 8, 128),
                vmem(5, 2, 4, 32, 128), vmem(32, 128),
                vmem(5, 2, 32, 128), vmem(5, 2, 32, 128), vmem(5, 16, 128), vmem(5, 2, 16, 128),
                vmem(128, 128), vmem(32, 128), vmem(16, 128), vmem(2, 8, 128), vmem(128, 128), vmem(16, 8, 128),
                pltpu.SemaphoreType.DMA((6,)), pltpu.SemaphoreType.DMA((5, 7)),
                pltpu.SemaphoreType.DMA((5, 7)), pltpu.SemaphoreType.DMA((2, 2)),
            ],
            compiler_params=pltpu.CompilerParams(
                collective_id=0, has_side_effects=True, vmem_limit_bytes=24 << 20
            ),
        )(start, rhs_block, coefficients)

    return jax.shard_map(local, mesh=mesh, in_specs=(spec,) * 3, out_specs=spec, check_vma=False)
```

time: 546 us -> 51.3 us (0.09)
  other arithmetic: 195 us -> 0 us
  blocking collectives: 116 us -> 0 us
  starting transfers between devices: 110 us -> 0 us
  local copies, waits for them, and re-layouts: 62.4 us -> 3.64 us
  Pallas kernels: 0 us -> 47.4 us
  between operations: 29.3 us -> 0.01 us
  matrix products: 20.1 us -> 0 us
  waiting for transfers between devices: 8.15 us -> 0 us
    div x4 -> x0, other arithmetic: 124 us -> none  [the longest x2 123 us: back_solve(): answer[i] = partial_sum / triangle[i, i]]
    psum x1 -> x0, blocking collectives: 116 us -> none  [local(): gram = lax.psum(local_gram, ('gx', 'gy', 'gz'))]
    ppermute x35 -> x0, starting transfers between devices: 110 us -> none  [the longest x18 81.2 us: padded(): lax.ppermute(lax.slice_in_dim(block, block.shape[dim] - width, None, axis...]
    pallas_call x0 -> x1, Pallas kernels: none -> 47.4 us  [local(): pl.pallas_call(lambda *refs: kernel(sizes, *refs), out_shape=jax.ShapeDty...]
    slice x82 -> x0, local copies, waits for them, and re-layouts: 35.5 us -> none  [the longest x20 11.6 us: reflect_rows(): leading = tall[j, j]]
    another operation x9 -> x0, other arithmetic: 26.9 us -> none  [the longest x1 19.3 us: back_solve(): return jnp.stack(answer)]
    reduce_sum x40 -> x0, other arithmetic: 25.7 us -> none  [the longest x20 13.6 us: reflect_rows(): length = jnp.sqrt(jnp.sum(column * column))]
    dot_general x23 -> x0, matrix products: 20.1 us -> none  [the longest x20 15.7 us: reflect_rows(): project = jnp.dot(tall, vector, precision=lax.Precision.HIGHEST) / weight]
  transfers between devices with their start and end apart: 35 -> 0, of which waited for: 8 -> 0; matrix products, arithmetic and copies ran while one was open for 6% -> 0% of each run, Pallas kernels for 0% -> 0%
where the time goes in v1:
time: 51.3 us; the launch traced here: 51.1 us
  Pallas kernels  47.4 us (92%)
  local copies, waits for them, and re-layouts  3.64 us (7%)
    pallas_call x1, Pallas kernels, local(): pl.pallas_call(lambda *refs: kernel(sizes, *refs), out_shape=jax.ShapeDty...  47.4 us
    unnamed x7, local copies, waits for them, and re-layouts  3.64 us

profile of v1, /device:TPU:1, one launch (start us, length us, event | category | flops | bytes accessed | tf_op | source)
XLA Modules:
  0.0 51.1 jit_solution(3536573008830389060)
XLA Ops:
  0.0 0.0 copy-start
  0.0 1.0 %copy-done = f32[4,5,32,128]{3,2,1,0:T(8,128)S(1)} copy-done((f32[4,5,32,128]{3,2,1,0:T(8,128)S(1)}, f32[4,5,32,128]{3,2,1,0:T(8,128)}, u32[]{:S(2)}) %copy-start) | copy-done | bytes 327704
  1.0 0.0 copy-start.1
  1.0 1.0 %copy-done.1 = f32[4,5,32,128]{3,2,1,0:T(8,128)S(1)} copy-done((f32[4,5,32,128]{3,2,1,0:T(8,128)S(1)}, f32[4,5,32,128]{3,2,1,0:T(8,128)}, u32[]{:S(2)}) %copy-start.1) | copy-done | bytes 327704
  1.9 0.0 copy-start.2
  1.9 1.0 %copy-done.2 = f32[4,5,32,128]{3,2,1,0:T(8,128)S(1)} copy-done((f32[4,5,32,128]{3,2,1,0:T(8,128)S(1)}, f32[4,5,32,128]{3,2,1,0:T(8,128)}, u32[]{:S(2)}) %copy-start.2) | copy-done | bytes 327704
  2.9 47.4 %shard_map.37 = f32[4,5,32,128]{3,2,1,0:T(8,128)S(1)} custom-call(f32[4,5,32,128]{3,2,1,0:T(8,128)S(1)} %copy-done, f32[4,5,32,128]{3,2,1,0:T(8,128)S(1)} %copy-done.1, f32[4,5,32,128]{3,2,1,0:T(8,128)S(1)} %copy-done.2), custom_call_target="tpu_custom_call" | custom-call | tf_op jit(solution)/shard_map/pallas_call | solution.py:367
  50.4 0.7 %copy.5 = f32[4,5,32,128]{3,2,1,0:T(8,128)} copy(f32[4,5,32,128]{3,2,1,0:T(8,128)S(1)} %shard_map.37) | data formatting | bytes 655360
Async XLA Ops:
  0.0 1.0 %copy-start = (f32[4,5,32,128]{3,2,1,0:T(8,128)S(1)}, f32[4,5,32,128]{3,2,1,0:T(8,128)}, u32[]{:S(2)}) copy-start(f32[4,5,32,128]{3,2,1,0:T(8,128)} %refs_0_.1) | copy-start | bytes 983044
  1.0 1.0 %copy-start.1 = (f32[4,5,32,128]{3,2,1,0:T(8,128)S(1)}, f32[4,5,32,128]{3,2,1,0:T(8,128)}, u32[]{:S(2)}) copy-start(f32[4,5,32,128]{3,2,1,0:T(8,128)} %refs_1_.1) | copy-start | bytes 983044
  1.9 1.0 %copy-start.2 = (f32[4,5,32,128]{3,2,1,0:T(8,128)S(1)}, f32[4,5,32,128]{3,2,1,0:T(8,128)}, u32[]{:S(2)}) copy-start(f32[4,5,32,128]{3,2,1,0:T(8,128)} %refs_2_.1) | copy-start | bytes 983044

commit v2 on v1

--- a/solution.py
+++ b/solution.py
@@ -9,7 +9,6 @@
 
 MESH = pl.DeviceIdType.MESH
 F32 = jnp.float32
-HIGH = lax.Precision.HIGHEST
 AXES = ("gx", "gy", "gz")
 SHIFT, SCALE = 8.75, 4.0
 PAIRS = [(i, j) for i in range(4) for j in range(i, 4)]
@@ -20,6 +19,15 @@
 
 def rolled(tile, shift):
     return pltpu.roll(tile, shift % 128, 1)
+
+
+def lane_sums(x):
+    high = x.astype(jnp.bfloat16)
+    rest = x - high.astype(F32)
+    middle = rest.astype(jnp.bfloat16)
+    low = (rest - middle.astype(F32)).astype(jnp.bfloat16)
+    terms = jnp.concatenate([low, middle, high], axis=1)
+    return jnp.dot(terms, jnp.ones((384, 128), jnp.bfloat16), preferred_element_type=F32)
 
 
 def kernel(
@@ -49,8 +57,11 @@
         copy.start()
 
     barrier = pltpu.get_barrier_semaphore()
-    partners = [shifted(o) for o in plane + line]
-    for partner in partners:
+    twin = me[0] + 1 - 2 * lax.rem(me[0], 2)
+    near = [(twin, me[1], me[2])] + [
+        (lax.rem(base + d, nx), me[1], me[2]) for base in (me[0], twin) for d in (2, nx - 2)
+    ] + neighbours[2:]
+    for partner in near:
         pl.semaphore_signal(barrier, inc=1, device_id=partner, device_id_type=MESH)
 
     lane = lax.broadcasted_iota(jnp.int32, (8, 128), 1)
@@ -64,6 +75,59 @@
 
     low = [inside(0, 0), inside(1, 0), inside(2, 0)]
     high = [inside(0, nx - 1), inside(1, ny - 1), inside(2, nz - 1)]
+
+    def x_copies(p):
+        return [
+            pltpu.make_async_remote_copy(
+                V.at[p, 4, :, pl.ds(TOP, 32), :], xh.at[p, 0], ssem.at[p, XLO], rsem.at[p, XLO],
+                device_id=neighbours[0], device_id_type=MESH),
+            pltpu.make_async_remote_copy(
+                V.at[p, 0, :, pl.ds(TOP, 32), :], xh.at[p, 1], ssem.at[p, XHI], rsem.at[p, XHI],
+                device_id=neighbours[1], device_id_type=MESH),
+        ]
+
+    def yz_copies(p):
+        return [
+            pltpu.make_async_remote_copy(
+                ys.at[p, d], yr.at[p, d], ssem.at[p, YLO + d], rsem.at[p, YLO + d],
+                device_id=neighbours[2 + d], device_id_type=MESH) for d in range(2)
+        ] + [
+            pltpu.make_async_remote_copy(
+                zs.at[p], zr.at[p, d], ssem.at[p, ZLO + d], rsem.at[p, ZLO + d],
+                device_id=neighbours[4 + d], device_id_type=MESH) for d in range(2)
+        ]
+
+    c_copy = pltpu.make_async_remote_copy(
+        coef_v.at[1, 4], c1h, ssem.at[0, CX], rsem.at[0, CX], device_id=neighbours[0], device_id_type=MESH
+    )
+
+    def begin(copies):
+        for copy in copies:
+            copy.start()
+
+    def pack(tile, spot, t, held):
+        k = 2 * spot + t % 2
+        held[t // 2] = jnp.where(pair_lane == k, rolled(tile, 2 * k + 1), held[t // 2])
+
+    for copy in loads[:5]:
+        copy.wait()
+    held = [zero, zero]
+    for x in range(5):
+        for f in range(4):
+            j = 4 * x + f
+            ys[0, 0, pl.ds(j, 1), :] = V[0, x, f, pl.ds(TOP + 31, 1), :]
+            ys[0, 1, pl.ds(j, 1), :] = V[0, x, f, pl.ds(TOP, 1), :]
+            for t in range(4):
+                pack(V[0, x, f, pl.ds(TOP + 8 * t, 8), :], j, t, held)
+        ys[0, 0, pl.ds(20 + x, 1), :] = coef_v[2, x, pl.ds(31, 1), :]
+        ys[0, 1, pl.ds(20 + x, 1), :] = coef_v[2, x, pl.ds(31, 1), :]
+        for t in range(4):
+            pack(coef_v[3, x, pl.ds(8 * t, 8), :], 20 + x, t, held)
+    for h in range(2):
+        zs[0, pl.ds(8 * h, 8), :] = held[h]
+
+    pl.semaphore_wait(barrier, len(near))
+    begin(x_copies(0) + [c_copy] + yz_copies(0))
 
     def clear(i, carry):
         for f in range(4):
@@ -75,9 +139,7 @@
     lax.fori_loop(0, 5, clear, 0)
     for x in range(5):
         bc2[x, pl.ds(0, 8), :] = zero
-    G[pl.ds(96, 32), :] = jnp.zeros((32, 128), F32)
-
-    loads[4].wait()
+    G[...] = zero
 
     for x in range(5):
         for t in range(4):
@@ -100,59 +162,6 @@
                 e1[1, rows, :] = n1 * high[0]
         e2[1, x, :, :] = jnp.where(sub == 7, bc2[x, pl.ds(TOP + 24, 8), :] * high[1], 0.0)
 
-    def x_copies(p):
-        return [
-            pltpu.make_async_remote_copy(
-                V.at[p, 4, :, pl.ds(TOP, 32), :], xh.at[p, 0], ssem.at[p, XLO], rsem.at[p, XLO],
-                device_id=neighbours[0], device_id_type=MESH),
-            pltpu.make_async_remote_copy(
-                V.at[p, 0, :, pl.ds(TOP, 32), :], xh.at[p, 1], ssem.at[p, XHI], rsem.at[p, XHI],
-                device_id=neighbours[1], device_id_type=MESH),
-        ]
-
-    def yz_copies(p):
-        return [
-            pltpu.make_async_remote_copy(
-                ys.at[p, d], yr.at[p, d], ssem.at[p, YLO + d], rsem.at[p, YLO + d],
-                device_id=neighbours[2 + d], device_id_type=MESH) for d in range(2)
-        ] + [
-            pltpu.make_async_remote_copy(
-                zs.at[p], zr.at[p, d], ssem.at[p, ZLO + d], rsem.at[p, ZLO + d],
-                device_id=neighbours[4 + d], device_id_type=MESH) for d in range(2)
-        ]
-
-    c_copy = pltpu.make_async_remote_copy(
-        coef_v.at[1, 4], c1h, ssem.at[0, CX], rsem.at[0, CX], device_id=neighbours[0], device_id_type=MESH
-    )
-
-    def begin(copies):
-        for copy in copies:
-            copy.start()
-
-    def pack(tile, spot, t, held):
-        k = 2 * spot + t % 2
-        held[t // 2] = jnp.where(pair_lane == k, rolled(tile, 2 * k + 1), held[t // 2])
-
-    for copy in loads[:4]:
-        copy.wait()
-    held = [zero, zero]
-    for x in range(5):
-        for f in range(4):
-            j = 4 * x + f
-            ys[0, 0, pl.ds(j, 1), :] = V[0, x, f, pl.ds(TOP + 31, 1), :]
-            ys[0, 1, pl.ds(j, 1), :] = V[0, x, f, pl.ds(TOP, 1), :]
-            for t in range(4):
-                pack(V[0, x, f, pl.ds(TOP + 8 * t, 8), :], j, t, held)
-        ys[0, 0, pl.ds(20 + x, 1), :] = coef_v[2, x, pl.ds(31, 1), :]
-        ys[0, 1, pl.ds(20 + x, 1), :] = coef_v[2, x, pl.ds(31, 1), :]
-        for t in range(4):
-            pack(coef_v[3, x, pl.ds(8 * t, 8), :], 20 + x, t, held)
-    for h in range(2):
-        zs[0, pl.ds(8 * h, 8), :] = held[h]
-
-    pl.semaphore_wait(barrier, len(partners))
-    begin(x_copies(0) + [c_copy] + yz_copies(0))
-
     def interior(p):
         def layer(x, below, above):
             for t in range(4):
@@ -194,8 +203,11 @@
             return tuple(sums)
 
         sums = lax.fori_loop(0, 5, layer, (zero,) * 20)
+        totals = lane_sums(jnp.concatenate(sums, axis=0))
+        block = G[...]
         for q in range(20):
-            G[pl.ds(20 * p - 20 + q, 1), :] = jnp.sum(sums[q], axis=0, keepdims=True)
+            block = jnp.where(lane == 20 * p - 20 + q, totals[8 * q : 8 * q + 8, :], block)
+        G[...] = block
 
     def finish(p, first=False, last=False):
         for copy in x_copies(p) + yz_copies(p) + ([c_copy] if first else []):
@@ -272,8 +284,6 @@
     finish(4, last=True)
     products(5)
 
-    ones = jnp.ones((8, 128), F32)
-
     def everyone(row, offsets, rows_ref, mine, count, slot):
         msg[slot, :, :] = row
         copies = [
@@ -294,7 +304,7 @@
         others = rows_ref.at[pl.ds(0, count - 1), :]
         pltpu.make_async_copy(others, others, asem.at[slot, 0]).wait()
 
-    g = lax.dot_general(ones, G[...], (((1,), (1,)), ((), ())), precision=HIGH, preferred_element_type=F32)
+    g = jnp.broadcast_to(jnp.sum(G[...], axis=0, keepdims=True), (8, 128))
     g = everyone(g, plane, row_a, me[1] * nz + me[2], ny * nz, 0)
     g = everyone(g, line, row_b, me[0], nx, 1)
 
@@ -303,9 +313,7 @@
     right = SHIFT * g + SCALE * ahead
     entries = jnp.where(lane < 80, normal, rolled(right, 70))
     spread = jnp.concatenate([jnp.where(sub + 8 * r == lane, entries, 0.0) for r in range(16)], axis=0)
-    rep[...] = lax.dot_general(
-        spread, jnp.ones((128, 128), F32), (((1,), (0,)), ((), ())), precision=HIGH, preferred_element_type=F32
-    )
+    rep[...] = lane_sums(spread)
 
     def entry(r):
         return jnp.broadcast_to(rep[pl.ds(r, 1), :], (8, 128))
@@ -376,12 +384,12 @@
                 vmem(2, 32, 128), vmem(2, 5, 8, 128),
                 vmem(5, 2, 4, 32, 128), vmem(32, 128),
                 vmem(5, 2, 32, 128), vmem(5, 2, 32, 128), vmem(5, 16, 128), vmem(5, 2, 16, 128),
-                vmem(128, 128), vmem(32, 128), vmem(16, 128), vmem(2, 8, 128), vmem(128, 128), vmem(16, 8, 128),
+                vmem(8, 128), vmem(32, 128), vmem(16, 128), vmem(2, 8, 128), vmem(128, 128), vmem(16, 8, 128),
                 pltpu.SemaphoreType.DMA((6,)), pltpu.SemaphoreType.DMA((5, 7)),
                 pltpu.SemaphoreType.DMA((5, 7)), pltpu.SemaphoreType.DMA((2, 2)),
             ],
             compiler_params=pltpu.CompilerParams(
-                collective_id=0, has_side_effects=True, vmem_limit_bytes=24 << 20
+                collective_id=0, has_side_effects=True, vmem_limit_bytes=60 << 20
             ),
         )(start, rhs_block, coefficients)
 

time: 51.3 us -> 46.6 us (0.908)
  Pallas kernels: 47.4 us -> 44.7 us
  local copies, waits for them, and re-layouts: 3.64 us -> 1.72 us
    pallas_call x1, Pallas kernels: 47.4 us -> 44.7 us  [local(): pl.pallas_call(lambda *refs: kernel(sizes, *refs), out_shape=jax.ShapeDty...]
    unnamed x7 -> x1, local copies, waits for them, and re-layouts: 3.64 us -> 1.72 us
where the time goes in v2:
time: 46.6 us; the launch traced here: 46.4 us
  Pallas kernels  44.7 us (96%)
  local copies, waits for them, and re-layouts  1.72 us (4%)
    pallas_call x1, Pallas kernels, local(): pl.pallas_call(lambda *refs: kernel(sizes, *refs), out_shape=jax.ShapeDty...  44.7 us
    unnamed x1, local copies, waits for them, and re-layouts  1.72 us

profile of v2, /device:TPU:1, one launch (start us, length us, event | category | flops | bytes accessed | tf_op | source)
XLA Modules:
  0.0 46.4 jit_solution(244364397153445660)
XLA Ops:
  0.0 44.7 %shard_map.37 = f32[4,5,32,128]{3,2,1,0:T(8,128)} custom-call(f32[4,5,32,128]{3,2,1,0:T(8,128)} %refs_0_.1, f32[4,5,32,128]{3,2,1,0:T(8,128)} %refs_1_.1, f32[4,5,32,128]{3,2,1,0:T(8,128)} %refs_2_.1), custom_call_target="tpu_custom_call" | custom-call | tf_op jit(solution)/shard_map/pallas_call | solution.py:375
  44.7 1.7 %copy.5 = f32[4,5,32,128]{3,2,1,0:T(8,128)} copy(f32[4,5,32,128]{3,2,1,0:T(8,128)} %shard_map.37) | data formatting | bytes 655360

commit v3 on v2

--- a/solution.py
+++ b/solution.py
@@ -14,7 +14,8 @@
 PAIRS = [(i, j) for i in range(4) for j in range(i, 4)]
 PLACE = {(i, j): PAIRS.index((min(i, j), max(i, j))) for i in range(4) for j in range(4)}
 TOP = 8
-XLO, XHI, YLO, YHI, ZLO, ZHI, CX = range(7)
+XLO, XHI, YLO, YHI, ZLO, ZHI = range(6)
+YF, ZF = 8, 10
 
 
 def rolled(tile, shift):
@@ -33,14 +34,20 @@
 def kernel(
     sizes, start, rhs, coef, out,
     V, rhs_v, coef_v, bd, bc1, bc2, bc3p, bc3m, e3, e1, e2,
-    xh, c1h, ys, yr, zs, zr, G, row_a, row_b, msg, rep, W,
+    faces, c1h, ys, zs, G, parts, row_a, row_b, msg, rep, W,
     lsem, ssem, rsem, asem,
 ):
     nx, ny, nz = sizes
     me = [lax.axis_index(axis) for axis in AXES]
 
+    def ahead_by(axis, d):
+        place = me[axis] + d
+        return place if d == 0 else jnp.where(place >= sizes[axis], place - sizes[axis], place)
+
+    places = [[ahead_by(axis, d) for d in range(sizes[axis])] for axis in range(3)]
+
     def shifted(offset):
-        return tuple(lax.rem(m + (d + s), s) for m, d, s in zip(me, offset, sizes))
+        return tuple(places[axis][d % sizes[axis]] for axis, d in enumerate(offset))
 
     neighbours = [shifted(o) for o in ((1, 0, 0), (-1, 0, 0), (0, 1, 0), (0, -1, 0), (0, 0, 1), (0, 0, -1))]
 
@@ -49,6 +56,14 @@
 
     plane = sorted([(0, b, c) for b, c in itertools.product(range(ny), range(nz)) if b or c], key=far)
     line = sorted([(a, 0, 0) for a in range(1, nx)], key=far)
+
+    barrier = pltpu.get_barrier_semaphore()
+    twin = me[0] + 1 - 2 * lax.rem(me[0], 2)
+    near = [(twin, me[1], me[2])] + [
+        (jnp.where(base + d >= nx, base + d - nx, base + d), me[1], me[2]) for base in (me[0], twin) for d in (2, nx - 2)
+    ] + neighbours[2:]
+    for partner in near:
+        pl.semaphore_signal(barrier, inc=1, device_id=partner, device_id_type=MESH)
 
     loads = [
         pltpu.make_async_copy(start.at[f], V.at[0, :, f, pl.ds(TOP, 32), :], lsem.at[f]) for f in range(4)
@@ -56,14 +71,6 @@
     for copy in loads:
         copy.start()
 
-    barrier = pltpu.get_barrier_semaphore()
-    twin = me[0] + 1 - 2 * lax.rem(me[0], 2)
-    near = [(twin, me[1], me[2])] + [
-        (lax.rem(base + d, nx), me[1], me[2]) for base in (me[0], twin) for d in (2, nx - 2)
-    ] + neighbours[2:]
-    for partner in near:
-        pl.semaphore_signal(barrier, inc=1, device_id=partner, device_id_type=MESH)
-
     lane = lax.broadcasted_iota(jnp.int32, (8, 128), 1)
     sub = lax.broadcasted_iota(jnp.int32, (8, 128), 0)
     pair_lane = lax.shift_right_logical(lane, 1)
@@ -76,29 +83,26 @@
     low = [inside(0, 0), inside(1, 0), inside(2, 0)]
     high = [inside(0, nx - 1), inside(1, ny - 1), inside(2, nz - 1)]
 
+    def send(source, target, p, way):
+        return pltpu.make_async_remote_copy(
+            source, target, ssem.at[p], rsem.at[p], device_id=neighbours[way], device_id_type=MESH
+        )
+
     def x_copies(p):
         return [
-            pltpu.make_async_remote_copy(
-                V.at[p, 4, :, pl.ds(TOP, 32), :], xh.at[p, 0], ssem.at[p, XLO], rsem.at[p, XLO],
-                device_id=neighbours[0], device_id_type=MESH),
-            pltpu.make_async_remote_copy(
-                V.at[p, 0, :, pl.ds(TOP, 32), :], xh.at[p, 1], ssem.at[p, XHI], rsem.at[p, XHI],
-                device_id=neighbours[1], device_id_type=MESH),
+            send(V.at[p, 4 - 4 * d, :, pl.ds(TOP, 32), :], faces.at[p, pl.ds(4 * d, 4)], p, XLO + d) for d in range(2)
         ]
 
     def yz_copies(p):
-        return [
-            pltpu.make_async_remote_copy(
-                ys.at[p, d], yr.at[p, d], ssem.at[p, YLO + d], rsem.at[p, YLO + d],
-                device_id=neighbours[2 + d], device_id_type=MESH) for d in range(2)
-        ] + [
-            pltpu.make_async_remote_copy(
-                zs.at[p], zr.at[p, d], ssem.at[p, ZLO + d], rsem.at[p, ZLO + d],
-                device_id=neighbours[4 + d], device_id_type=MESH) for d in range(2)
+        return [send(ys.at[p, d], faces.at[p, YF + d], p, YLO + d) for d in range(2)] + [
+            send(zs.at[p], faces.at[p, ZF, pl.ds(16 * d, 16), :], p, ZLO + d) for d in range(2)
         ]
 
+    def all_six(p, sem):
+        pltpu.make_async_copy(faces.at[p], faces.at[p], sem.at[p]).wait()
+
     c_copy = pltpu.make_async_remote_copy(
-        coef_v.at[1, 4], c1h, ssem.at[0, CX], rsem.at[0, CX], device_id=neighbours[0], device_id_type=MESH
+        coef_v.at[1, 4], c1h, ssem.at[5], rsem.at[5], device_id=neighbours[0], device_id_type=MESH
     )
 
     def begin(copies):
@@ -140,6 +144,7 @@
     for x in range(5):
         bc2[x, pl.ds(0, 8), :] = zero
     G[...] = zero
+    parts[pl.ds(160, 32), :] = jnp.zeros((32, 128), F32)
 
     for x in range(5):
         for t in range(4):
@@ -203,17 +208,26 @@
             return tuple(sums)
 
         sums = lax.fori_loop(0, 5, layer, (zero,) * 20)
-        totals = lane_sums(jnp.concatenate(sums, axis=0))
+        for q in range(20):
+            parts[pl.ds(8 * q, 8), :] = sums[q]
+        rows = parts[pl.ds(0, 24, stride=8), :]
+        for r in range(1, 8):
+            rows = rows + parts[pl.ds(r, 24, stride=8), :]
+        totals = lane_sums(rows)
         block = G[...]
-        for q in range(20):
-            block = jnp.where(lane == 20 * p - 20 + q, totals[8 * q : 8 * q + 8, :], block)
+        for h in range(3):
+            mine = lane == sub + (20 * p - 20 + 8 * h)
+            if h == 2:
+                mine = mine & (sub < 4)
+            block = block + jnp.where(mine, totals[8 * h : 8 * h + 8, :], 0.0)
         G[...] = block
 
     def finish(p, first=False, last=False):
-        for copy in x_copies(p) + yz_copies(p) + ([c_copy] if first else []):
-            copy.wait_recv()
+        all_six(p, rsem)
+        if first:
+            c_copy.wait_recv()
         both = [
-            jnp.where(even_lane, zr[p, 0, pl.ds(8 * h, 8), :], rolled(zr[p, 1, pl.ds(8 * h, 8), :], -2))
+            jnp.where(even_lane, faces[p, ZF, pl.ds(8 * h, 8), :], rolled(faces[p, ZF, pl.ds(16 + 8 * h, 8), :], -2))
             for h in range(2)
         ]
         held = [zero, zero]
@@ -231,7 +245,7 @@
                         e1[0, rows, :] = face
                         more = more + face
                     if t == 0:
-                        row = jnp.broadcast_to(yr[p, 0, pl.ds(20 + x, 1), :], (8, 128))
+                        row = jnp.broadcast_to(faces[p, YF, pl.ds(20 + x, 1), :], (8, 128))
                         face = jnp.where(sub == 0, (-0.25 * low[1]) * row, 0.0)
                         e2[0, x, :, :] = face
                         more = more + face
@@ -242,13 +256,13 @@
                     cells = pl.ds(TOP + 8 * t, 8)
                     total = V[p + 1, x, f, cells, :]
                     if x == 0:
-                        total = total + e1[0, rows, :] * xh[p, 0, f, rows, :]
+                        total = total + e1[0, rows, :] * faces[p, f, rows, :]
                     if x == 4:
-                        total = total + e1[1, rows, :] * xh[p, 1, f, rows, :]
+                        total = total + e1[1, rows, :] * faces[p, 4 + f, rows, :]
                     if t == 0:
-                        total = total + e2[0, x, :, :] * jnp.broadcast_to(yr[p, 0, pl.ds(j, 1), :], (8, 128))
+                        total = total + e2[0, x, :, :] * jnp.broadcast_to(faces[p, YF, pl.ds(j, 1), :], (8, 128))
                     if t == 3:
-                        total = total + e2[1, x, :, :] * jnp.broadcast_to(yr[p, 1, pl.ds(j, 1), :], (8, 128))
+                        total = total + e2[1, x, :, :] * jnp.broadcast_to(faces[p, YF + 1, pl.ds(j, 1), :], (8, 128))
                     total = total + edge * rolled(both[t // 2], -2 * k)
                     if first:
                         v = V[p, x, f, cells, :]
@@ -284,7 +298,7 @@
     finish(4, last=True)
     products(5)
 
-    def everyone(row, offsets, rows_ref, mine, count, slot):
+    def everyone(row, offsets, rows_ref, mine, count, slot, meanwhile):
         msg[slot, :, :] = row
         copies = [
             pltpu.make_async_remote_copy(
@@ -292,6 +306,7 @@
                 device_id=shifted(o), device_id_type=MESH) for o in offsets
         ]
         begin(copies)
+        meanwhile()
         others = rows_ref.at[pl.ds(0, count - 1), :]
         pltpu.make_async_copy(others, others, asem.at[slot, 1]).wait()
         total = None
@@ -305,8 +320,13 @@
         pltpu.make_async_copy(others, others, asem.at[slot, 0]).wait()
 
     g = jnp.broadcast_to(jnp.sum(G[...], axis=0, keepdims=True), (8, 128))
-    g = everyone(g, plane, row_a, me[1] * nz + me[2], ny * nz, 0)
-    g = everyone(g, line, row_b, me[0], nx, 1)
+    def faces_sent():
+        for p in range(5):
+            all_six(p, ssem)
+        c_copy.wait_send()
+
+    g = everyone(g, plane, row_a, me[1] * nz + me[2], ny * nz, 0, faces_sent)
+    g = everyone(g, line, row_b, me[0], nx, 1, lambda: sent(row_a, ny * nz, 0))
 
     ahead, after = rolled(g, -10), rolled(g, -20)
     normal = (SHIFT * SHIFT) * g + (2 * SHIFT * SCALE) * ahead + (SCALE * SCALE) * after
@@ -358,11 +378,6 @@
 
     lax.fori_loop(0, 5, update, 0)
 
-    for p in range(5):
-        for copy in x_copies(p) + yz_copies(p):
-            copy.wait_send()
-    c_copy.wait_send()
-    sent(row_a, ny * nz, 0)
     sent(row_b, nx, 1)
 
 
@@ -382,14 +397,14 @@
                 vmem(5, 32, 128), vmem(5, 32, 128), vmem(5, 48, 128),
                 vmem(5, 32, 128), vmem(5, 32, 128), vmem(5, 32, 128),
                 vmem(2, 32, 128), vmem(2, 5, 8, 128),
-                vmem(5, 2, 4, 32, 128), vmem(32, 128),
-                vmem(5, 2, 32, 128), vmem(5, 2, 32, 128), vmem(5, 16, 128), vmem(5, 2, 16, 128),
-                vmem(8, 128), vmem(32, 128), vmem(16, 128), vmem(2, 8, 128), vmem(128, 128), vmem(16, 8, 128),
-                pltpu.SemaphoreType.DMA((6,)), pltpu.SemaphoreType.DMA((5, 7)),
-                pltpu.SemaphoreType.DMA((5, 7)), pltpu.SemaphoreType.DMA((2, 2)),
+                vmem(5, 11, 32, 128), vmem(32, 128),
+                vmem(5, 2, 32, 128), vmem(5, 16, 128),
+                vmem(8, 128), vmem(192, 128), vmem(32, 128), vmem(16, 128), vmem(2, 8, 128), vmem(128, 128), vmem(16, 8, 128),
+                pltpu.SemaphoreType.DMA((6,)), pltpu.SemaphoreType.DMA((6,)),
+                pltpu.SemaphoreType.DMA((6,)), pltpu.SemaphoreType.DMA((2, 2)),
             ],
             compiler_params=pltpu.CompilerParams(
-                collective_id=0, has_side_effects=True, vmem_limit_bytes=60 << 20
+                collective_id=0, has_side_effects=True, vmem_limit_bytes=54764 << 10
             ),
         )(start, rhs_block, coefficients)
 

time: 46.6 us -> 44.3 us (0.951)
  Pallas kernels: 44.7 us -> 43.4 us
  local copies, waits for them, and re-layouts: 1.72 us -> 0.73 us
    pallas_call x1, Pallas kernels: 44.7 us -> 43.4 us  [local(): pl.pallas_call(lambda *refs: kernel(sizes, *refs), out_shape=jax.ShapeDty...]
    unnamed x1, local copies, waits for them, and re-layouts: 1.72 us -> 0.73 us
where the time goes in v3:
time: 44.3 us; the launch traced here: 44.1 us
  Pallas kernels  43.4 us (98%)
  local copies, waits for them, and re-layouts  0.73 us (2%)
    pallas_call x1, Pallas kernels, local(): pl.pallas_call(lambda *refs: kernel(sizes, *refs), out_shape=jax.ShapeDty...  43.4 us

profile of v3, /device:TPU:1, one launch (start us, length us, event | category | flops | bytes accessed | tf_op | source)
XLA Modules:
  0.0 44.1 jit_solution(14946469698900786612)
XLA Ops:
  0.0 43.4 %shard_map.37 = f32[4,5,32,128]{3,2,1,0:T(8,128)S(1)} custom-call(f32[4,5,32,128]{3,2,1,0:T(8,128)} %refs_0_.1, f32[4,5,32,128]{3,2,1,0:T(8,128)} %refs_1_.1, f32[4,5,32,128]{3,2,1,0:T(8,128)} %refs_2_.1), custom_call_target="tpu_custom_call" | custom-call | tf_op jit(solution)/shard_map/pallas_call | solution.py:390
  43.4 0.7 %copy.5 = f32[4,5,32,128]{3,2,1,0:T(8,128)} copy(f32[4,5,32,128]{3,2,1,0:T(8,128)S(1)} %shard_map.37) | data formatting | bytes 655360

commit v4 on v3

--- a/solution.py
+++ b/solution.py
@@ -34,7 +34,7 @@
 def kernel(
     sizes, start, rhs, coef, out,
     V, rhs_v, coef_v, bd, bc1, bc2, bc3p, bc3m, e3, e1, e2,
-    faces, c1h, ys, zs, G, parts, row_a, row_b, msg, rep, W,
+    faces, c1h, ys, zs, G, parts, row_a, row_b, msg, W,
     lsem, ssem, rsem, asem,
 ):
     nx, ny, nz = sizes
@@ -59,9 +59,10 @@
 
     barrier = pltpu.get_barrier_semaphore()
     twin = me[0] + 1 - 2 * lax.rem(me[0], 2)
-    near = [(twin, me[1], me[2])] + [
-        (jnp.where(base + d >= nx, base + d - nx, base + d), me[1], me[2]) for base in (me[0], twin) for d in (2, nx - 2)
-    ] + neighbours[2:]
+    near = neighbours[2:] + [
+        (jnp.where(base + d >= nx, base + d - nx, base + d), me[1], me[2])
+        for base in (twin, me[0]) for d in (2, nx - 2)
+    ] + [(twin, me[1], me[2])]
     for partner in near:
         pl.semaphore_signal(barrier, inc=1, device_id=partner, device_id_type=MESH)
 
@@ -131,7 +132,7 @@
         zs[0, pl.ds(8 * h, 8), :] = held[h]
 
     pl.semaphore_wait(barrier, len(near))
-    begin(x_copies(0) + [c_copy] + yz_copies(0))
+    begin(yz_copies(0) + x_copies(0) + [c_copy])
 
     def clear(i, carry):
         for f in range(4):
@@ -167,7 +168,7 @@
                 e1[1, rows, :] = n1 * high[0]
         e2[1, x, :, :] = jnp.where(sub == 7, bc2[x, pl.ds(TOP + 24, 8), :] * high[1], 0.0)
 
-    def interior(p):
+    def interior(p, first=False):
         def layer(x, below, above):
             for t in range(4):
                 rows = pl.ds(8 * t, 8)
@@ -185,6 +186,8 @@
                         total = total + bc1[x - 1, rows, :] * V[p, x - 1, f, pl.ds(TOP + 8 * t, 8), :]
                     total = total + c_zp * rolled(v, -1)
                     total = total + c_zm * rolled(v, 1)
+                    if first:
+                        total = rhs_v[f, x, rows, :] - SHIFT * v - SCALE * total
                     V[p + 1, x, f, pl.ds(TOP + 8 * t, 8), :] = total
 
         layer(0, False, True)
@@ -254,7 +257,7 @@
                     j = 4 * x + f
                     k = 2 * j + t % 2
                     cells = pl.ds(TOP + 8 * t, 8)
-                    total = V[p + 1, x, f, cells, :]
+                    total = -more * V[p, x, f, cells, :] if first else V[p + 1, x, f, cells, :]
                     if x == 0:
                         total = total + e1[0, rows, :] * faces[p, f, rows, :]
                     if x == 4:
@@ -265,9 +268,7 @@
                         total = total + e2[1, x, :, :] * jnp.broadcast_to(faces[p, YF + 1, pl.ds(j, 1), :], (8, 128))
                     total = total + edge * rolled(both[t // 2], -2 * k)
                     if first:
-                        v = V[p, x, f, cells, :]
-                        total = total - more * v
-                        total = rhs_v[f, x, rows, :] - SHIFT * v - SCALE * total
+                        total = V[p + 1, x, f, cells, :] - SCALE * total
                     V[p + 1, x, f, cells, :] = total
                     if not last:
                         if t == 3:
@@ -282,8 +283,8 @@
                 zs[p + 1, pl.ds(8 * h, 8), :] = held[h]
             begin(yz_copies(p + 1))
 
-    interior(0)
     loads[5].wait()
+    interior(0, first=True)
     finish(0, first=True)
 
     def power(p, carry):
@@ -325,18 +326,15 @@
             all_six(p, ssem)
         c_copy.wait_send()
 
-    g = everyone(g, plane, row_a, me[1] * nz + me[2], ny * nz, 0, faces_sent)
-    g = everyone(g, line, row_b, me[0], nx, 1, lambda: sent(row_a, ny * nz, 0))
+    g = everyone(g, line, row_b, me[0], nx, 1, faces_sent)
+    g = everyone(g, plane, row_a, me[1] * nz + me[2], ny * nz, 0, lambda: sent(row_b, nx, 1))
 
     ahead, after = rolled(g, -10), rolled(g, -20)
     normal = (SHIFT * SHIFT) * g + (2 * SHIFT * SCALE) * ahead + (SCALE * SCALE) * after
     right = SHIFT * g + SCALE * ahead
     entries = jnp.where(lane < 80, normal, rolled(right, 70))
-    spread = jnp.concatenate([jnp.where(sub + 8 * r == lane, entries, 0.0) for r in range(16)], axis=0)
-    rep[...] = lane_sums(spread)
-
     def entry(r):
-        return jnp.broadcast_to(rep[pl.ds(r, 1), :], (8, 128))
+        return jnp.broadcast_to(entries[:, r : r + 1], (8, 128))
 
     n = 16
     a = {}
@@ -378,7 +376,7 @@
 
     lax.fori_loop(0, 5, update, 0)
 
-    sent(row_b, nx, 1)
+    sent(row_a, ny * nz, 0)
 
 
 def solution(mesh):
@@ -399,7 +397,7 @@
                 vmem(2, 32, 128), vmem(2, 5, 8, 128),
                 vmem(5, 11, 32, 128), vmem(32, 128),
                 vmem(5, 2, 32, 128), vmem(5, 16, 128),
-                vmem(8, 128), vmem(192, 128), vmem(32, 128), vmem(16, 128), vmem(2, 8, 128), vmem(128, 128), vmem(16, 8, 128),
+                vmem(8, 128), vmem(192, 128), vmem(32, 128), vmem(16, 128), vmem(2, 8, 128), vmem(16, 8, 128),
                 pltpu.SemaphoreType.DMA((6,)), pltpu.SemaphoreType.DMA((6,)),
                 pltpu.SemaphoreType.DMA((6,)), pltpu.SemaphoreType.DMA((2, 2)),
             ],

time: 44.3 us -> 43.3 us (0.977)
  Pallas kernels: 43.4 us -> 42.5 us
    pallas_call x1, Pallas kernels: 43.4 us -> 42.5 us  [local(): pl.pallas_call(lambda *refs: kernel(sizes, *refs), out_shape=jax.ShapeDty...]
where the time goes in v4:
time: 43.3 us; the launch traced here: 43.2 us
  Pallas kernels  42.5 us (98%)
  local copies, waits for them, and re-layouts  0.73 us (2%)
    pallas_call x1, Pallas kernels, local(): pl.pallas_call(lambda *refs: kernel(sizes, *refs), out_shape=jax.ShapeDty...  42.5 us

profile of v4, /device:TPU:1, one launch (start us, length us, event | category | flops | bytes accessed | tf_op | source)
XLA Modules:
  0.0 43.2 jit_solution(6459612593348309143)
XLA Ops:
  0.0 42.5 %shard_map.37 = f32[4,5,32,128]{3,2,1,0:T(8,128)S(1)} custom-call(f32[4,5,32,128]{3,2,1,0:T(8,128)} %refs_0_.1, f32[4,5,32,128]{3,2,1,0:T(8,128)} %refs_1_.1, f32[4,5,32,128]{3,2,1,0:T(8,128)} %refs_2_.1), custom_call_target="tpu_custom_call" | custom-call | tf_op jit(solution)/shard_map/pallas_call | solution.py:388
  42.5 0.7 %copy.5 = f32[4,5,32,128]{3,2,1,0:T(8,128)} copy(f32[4,5,32,128]{3,2,1,0:T(8,128)S(1)} %shard_map.37) | data formatting | bytes 655360

commit v5 on v4

--- a/solution.py
+++ b/solution.py
@@ -276,8 +276,8 @@
                         if t == 0:
                             ys[p + 1, 1, pl.ds(j, 1), :] = total[0:1, :]
                         pack(total, j, t, held)
-            if x == 4 and not last:
-                begin(x_copies(p + 1))
+            if x in (0, 4) and not last:
+                begin([x_copies(p + 1)[1 - x // 4]])
         if not last:
             for h in range(2):
                 zs[p + 1, pl.ds(8 * h, 8), :] = held[h]

time: 43.3 us -> 43.3 us (level)
  no operation moved by 1% of the time
where the time goes in v5:
time: 43.3 us; the launch traced here: 43.2 us
  Pallas kernels  42.5 us (98%)
  local copies, waits for them, and re-layouts  0.73 us (2%)
    pallas_call x1, Pallas kernels, local(): pl.pallas_call(lambda *refs: kernel(sizes, *refs), out_shape=jax.ShapeDty...  42.5 us

profile of v5, /device:TPU:1, one launch (start us, length us, event | category | flops | bytes accessed | tf_op | source)
XLA Modules:
  0.0 43.2 jit_solution(14097851485073264081)
XLA Ops:
  0.0 42.5 %shard_map.37 = f32[4,5,32,128]{3,2,1,0:T(8,128)S(1)} custom-call(f32[4,5,32,128]{3,2,1,0:T(8,128)} %refs_0_.1, f32[4,5,32,128]{3,2,1,0:T(8,128)} %refs_1_.1, f32[4,5,32,128]{3,2,1,0:T(8,128)} %refs_2_.1), custom_call_target="tpu_custom_call" | custom-call | tf_op jit(solution)/shard_map/pallas_call | solution.py:388
  42.5 0.7 %copy.5 = f32[4,5,32,128]{3,2,1,0:T(8,128)} copy(f32[4,5,32,128]{3,2,1,0:T(8,128)S(1)} %shard_map.37) | data formatting | bytes 655360
